TPU v7x, 32 devices: a whole 2x2x4 slice. The times are simulated.
32 devices in a mesh: leaf: 4 (over z), front: 8 (over y, x, core).
Axes of the slice: x: 2, y: 2, z: 4, core: 2. Of those that a mesh axis runs over, the one named last changes fastest.
Arguments:
- stacked: float32 [8, 4096, 896], P('front', 'leaf'), may hold values from -2.34375 to 2.34375, as said below
- row_owner: int32 [8, 640, 1], P('front', 'leaf'), may hold values from 0 to 7; in each aligned block of 160 rows (0 to 159, 160 to 319, ..., all dimensions but the last counted through in order) at most 40 rows name the same one
- dest_local: int32 [8, 640], P('front', 'leaf'), may hold values from 0 to 63
Outputs:
- pivot_rows: float32 [8, 256, 896], P('front', 'leaf')
- assembled: float32 [8, 256, 640], P('front', 'leaf')
Inputs may be any that keep to these rules, and one draw needn't show every extreme that they name: `stacked`: entries of a front's rows carry a scale of their row and one of their column. `row_owner`: among the 160 contribution rows of a front on one leaf index, no owner is named by more than 40 of them.
All inputs are finite; a program needn't handle non-finite values.
Results may differ from a plain program's by a relative error of at most 0.000076.
Values sent between devices are 32-bit elements; how exact they have to be, the bound alone decides.
A program may use at most 64 MiB of HBM per device.

v0:
```python
import functools
import jax
import jax.numpy as jnp
from jax import lax
from jax.experimental import pallas as pl
from jax.experimental.pallas import tpu as pltpu
from jax.sharding import PartitionSpec as P

PIV = 256
PR_DEV = 64
STRIP = 8
SUB = 32
PANEL = 128
CHUNK = 32
MESH = pl.DeviceIdType.MESH


highest = lax.Precision.HIGHEST


def factor_strip(a_ref, start, panel, strip, width):
    blocks = width // PANEL
    diag = a_ref[pl.ds(start, STRIP), pl.ds(pl.multiple_of(panel * PANEL, PANEL), PANEL)]
    c = {}
    for k in range(STRIP):
        lane = strip * STRIP + k
        column = jnp.broadcast_to(diag[:, lane:lane + 1], (STRIP, PANEL))
        for i in range(k, STRIP):
            c[i, k] = jnp.broadcast_to(column[i:i + 1, :], (STRIP, PANEL))
    body = [a_ref[pl.ds(start, STRIP), b * PANEL:(b + 1) * PANEL] for b in range(blocks)]
    body.append(diag)
    rows = [[jnp.broadcast_to(x[k:k + 1, :], (STRIP, PANEL)) for x in body] for k in range(STRIP)]
    for k in range(STRIP):
        inv = lax.rsqrt(c[k, k])
        rows[k] = [x * inv for x in rows[k]]
        for i in range(k + 1, STRIP):
            c[i, k] = c[i, k] * inv
        for i in range(k + 1, STRIP):
            for j in range(k + 1, i + 1):
                c[i, j] = c[i, j] - c[i, k] * c[j, k]
            rows[i] = [x - c[i, k] * y for x, y in zip(rows[i], rows[k])]
    sub = lax.broadcasted_iota(jnp.int32, (STRIP, PANEL), 0)
    lanes = lax.broadcasted_iota(jnp.int32, (STRIP, PANEL), 1)
    for b in range(blocks):
        out = rows[0][b]
        for k in range(1, STRIP):
            out = jnp.where(sub == k, rows[k][b], out)
        a_ref[pl.ds(start, STRIP), b * PANEL:(b + 1) * PANEL] = out
    return rows, sub, lanes


def one_hot_dot(picks, values):
    total = None
    for _ in range(3):
        piece = values.astype(jnp.bfloat16)
        values = values - piece.astype(jnp.float32)
        part = jnp.dot(picks, piece, preferred_element_type=jnp.float32)
        total = part if total is None else total + part
    return total


def front_kernel(
    x_ref, owner_ref, target_ref, pivot_ref, sum_ref, a_ref, update, select, dest_ref, high, low, own, in_l, in_r, out_l, out_r,
    rows_out, rows_in, dest_in, send_l, recv_l, send_r, recv_r, row_send, row_recv, dest_send, dest_recv,
):
    width = a_ref.shape[0]
    blocks = width // PANEL
    packed = (blocks + 1) // 2
    chunks = packed * PANEL // CHUNK
    per_panel = PANEL // CHUNK
    me, n = lax.axis_index("leaf"), lax.axis_size("leaf")
    has_left, has_right = me > 0, me < n - 1
    front, fronts = lax.axis_index("front"), lax.axis_size("front")
    slots, contrib_count = select.shape
    capacity = slots // fronts
    contrib_blocks = (width - PIV) // PANEL
    first_block = me * contrib_count // PANEL
    last_panel = (PIV + (me + 1) * contrib_count - 1) // PANEL
    peers = [lax.rem(front + d, fronts) for d in range(1, fronts)]

    barrier = pltpu.get_barrier_semaphore()

    @pl.when(has_left)
    def _():
        pl.semaphore_signal(barrier, inc=1, device_id={"leaf": me - 1}, device_id_type=MESH)

    @pl.when(has_right)
    def _():
        pl.semaphore_signal(barrier, inc=1, device_id={"leaf": me + 1}, device_id_type=MESH)

    rows_in[...] = jnp.zeros_like(rows_in)
    for peer in peers:
        pl.semaphore_signal(barrier, inc=1, device_id={"front": peer}, device_id_type=MESH)

    @pl.when(jnp.logical_not(has_left))
    def _():
        in_l[...] = jnp.zeros_like(in_l)

    @pl.when(jnp.logical_not(has_right))
    def _():
        in_r[...] = jnp.zeros_like(in_r)

    a_ref[...] = jnp.zeros_like(a_ref)
    update[...] = jnp.zeros_like(update)
    sum_ref[...] = jnp.zeros_like(sum_ref)
    high[...] = x_ref[...].astype(jnp.bfloat16)
    low[...] = (x_ref[...] - high[...].astype(jnp.float32)).astype(jnp.bfloat16)

    inner = jnp.logical_and(has_left, has_right)

    @pl.when(inner)
    def _():
        pl.semaphore_wait(barrier, 2 + fronts - 1)

    @pl.when(jnp.logical_not(inner))
    def _():
        pl.semaphore_wait(barrier, 1 + fronts - 1)

    def slots_of(g):
        return pl.ds(pl.multiple_of(g * capacity, STRIP), capacity)

    def dest_copy(to, src):
        return pltpu.make_async_remote_copy(
            src_ref=dest_ref.at[slots_of(to)], dst_ref=dest_in.at[slots_of(src)],
            send_sem=dest_send.at[to], recv_sem=dest_recv.at[src],
            device_id={"front": to}, device_id_type=MESH,
        )

    def row_copy(to, src, j):
        at = pl.ds(pl.multiple_of(j * PANEL, PANEL), PANEL)
        return pltpu.make_async_remote_copy(
            src_ref=rows_out.at[slots_of(to), at], dst_ref=rows_in.at[slots_of(src), at],
            send_sem=row_send.at[to, j], recv_sem=row_recv.at[src, j],
            device_id={"front": to}, device_id_type=MESH,
        )

    def send_rows():
        start = pl.multiple_of(PIV + me * contrib_count, STRIP)
        row = lax.broadcasted_iota(jnp.int32, (contrib_count, PANEL), 0) + me * contrib_count
        lane = lax.broadcasted_iota(jnp.int32, (contrib_count, PANEL), 1)

        def block(j, carry):
            at = pl.ds(pl.multiple_of(j * PANEL, PANEL), PANEL)
            rows = a_ref[pl.ds(start, contrib_count), pl.ds(pl.multiple_of(PIV + j * PANEL, PANEL), PANEL)]
            rows_out[:, at] = one_hot_dot(select[...], jnp.where(row <= lane + j * PANEL, rows, 0.0))
            for peer in peers:
                row_copy(peer, front, j).start()
            rows_in[slots_of(front), at] = rows_out[slots_of(front), at]
            return carry

        lax.fori_loop(first_block, contrib_blocks, block, 0)

    def prepare_slots():
        mine = jnp.broadcast_to(owner_ref[...].astype(jnp.float32), (contrib_count, PANEL))
        owner_row = mine.T[0:1, :]
        square = (contrib_count, contrib_count)
        before = lax.broadcasted_iota(jnp.int32, square, 0) < lax.broadcasted_iota(jnp.int32, square, 1)
        same = owner_ref[...].astype(jnp.float32) == owner_row
        rank = jnp.sum(jnp.where(same & before, 1.0, 0.0), axis=0, keepdims=True)
        slot_row = owner_row * capacity + rank
        chosen = lax.broadcasted_iota(jnp.int32, (slots, contrib_count), 0).astype(jnp.float32) == slot_row
        select[...] = jnp.where(chosen, 1.0, 0.0).astype(jnp.bfloat16)
        wanted = jnp.where(chosen, target_ref[...].astype(jnp.float32) + 1.0, 0.0)
        dest_ref[...] = jnp.broadcast_to(jnp.sum(wanted, axis=1, keepdims=True), dest_ref.shape)
        for peer in peers:
            dest_copy(peer, front).start()

    def rows_of(c):
        return pl.ds(pl.multiple_of(c * CHUNK, CHUNK), CHUNK)

    def to_right(src, c):
        return pltpu.make_async_remote_copy(
            src_ref=src.at[rows_of(c)], dst_ref=in_l.at[rows_of(c)],
            send_sem=send_r.at[c], recv_sem=recv_l.at[c],
            device_id={"leaf": me + 1}, device_id_type=MESH,
        )

    def to_left(src, c):
        return pltpu.make_async_remote_copy(
            src_ref=src.at[rows_of(c)], dst_ref=in_r.at[rows_of(c)],
            send_sem=send_l.at[c], recv_sem=recv_r.at[c],
            device_id={"leaf": me - 1}, device_id_type=MESH,
        )

    def from_left(c):
        @pl.when(has_left)
        def _():
            to_right(out_r, c).wait_recv()

            @pl.when(has_right)
            def _():
                out_r[rows_of(c), :] = own[rows_of(c), :] + in_l[rows_of(c), :]
                to_right(out_r, c).start()

    def from_right(c):
        @pl.when(has_right)
        def _():
            to_left(out_l, c).wait_recv()

            @pl.when(has_left)
            def _():
                out_l[rows_of(c), :] = own[rows_of(c), :] + in_r[rows_of(c), :]
                to_left(out_l, c).start()

    first_half = 2 * me < n

    def near(c):
        @pl.when(first_half)
        def _():
            from_left(c)

        @pl.when(jnp.logical_not(first_half))
        def _():
            from_right(c)

    def far(c):
        @pl.when(first_half)
        def _():
            from_right(c)

        @pl.when(jnp.logical_not(first_half))
        def _():
            from_left(c)

    def gram(panel, rows, at):
        cols = slice(panel * PANEL, (panel + 1) * PANEL)
        xt = x_ref[:, cols].T
        ht = xt.astype(jnp.bfloat16)
        lt = (xt - ht.astype(jnp.float32)).astype(jnp.bfloat16)
        right = slice(panel * PANEL, width)
        own[rows, at] = (
            jnp.dot(ht, high[:, right], preferred_element_type=jnp.float32)
            + jnp.dot(ht, low[:, right], preferred_element_type=jnp.float32)
            + jnp.dot(lt, high[:, right], preferred_element_type=jnp.float32)
        )

    def slot(k):
        if k <= per_panel:
            near(k)
            if k:
                far(k - 1)

    for q in range(packed):
        rows = slice(q * PANEL, (q + 1) * PANEL)
        gram(q, rows, slice(q * PANEL, width))
        if q:
            slot(2 * q - 2)
            gram(blocks - q, rows, slice(0, q * PANEL))

        @pl.when(jnp.logical_not(has_left))
        def _():
            for c in range(q * per_panel, (q + 1) * per_panel):
                to_right(own, c).start()

        @pl.when(jnp.logical_not(has_right))
        def _():
            for c in range(q * per_panel, (q + 1) * per_panel):
                to_left(own, c).start()

        if q:
            slot(2 * q - 1)
        else:
            prepare_slots()
    for k in range(2 * packed - 2, per_panel + 1):
        slot(k)

    def one_panel(panel, carry):
        base = pl.multiple_of(panel * PANEL, PANEL)
        folded = panel >= packed
        source = pl.ds(pl.multiple_of(jnp.where(folded, blocks - panel, panel) * PANEL, PANEL), PANEL)
        shift = jnp.where(folded, panel, 0)

        def total(j, carry):
            at = pl.ds(pl.multiple_of((j - shift) * PANEL, PANEL), PANEL)
            a_ref[pl.ds(base, PANEL), pl.ds(pl.multiple_of(j * PANEL, PANEL), PANEL)] = (
                own[source, at] + in_l[source, at] + in_r[source, at]
            ) - update[:, pl.ds(pl.multiple_of(j * PANEL, PANEL), PANEL)]
            return carry

        lax.fori_loop(panel, blocks, total, 0)

        @pl.when(panel > 0)
        def _():
            done = pl.ds(pl.multiple_of(base - PANEL, PANEL), PANEL)
            head = a_ref[done, pl.ds(base, PANEL)].T
            a_ref[pl.ds(base, PANEL), :] = a_ref[pl.ds(base, PANEL), :] - jnp.dot(
                head, a_ref[done, :], precision=lax.Precision.HIGH, preferred_element_type=jnp.float32
            )

        following = pl.multiple_of(jnp.minimum(panel + 1, blocks - 1) * PANEL, PANEL)
        batch = -(-(blocks - 1) // (PANEL // SUB)) * PANEL
        for group in range(PANEL // SUB):
            for part in range(SUB // CHUNK):
                c = (panel + 1) * per_panel + group * (SUB // CHUNK) + part

                @pl.when(c + 1 < chunks)
                def _():
                    near(c + 1)

                @pl.when(c < chunks)
                def _():
                    far(c)

            if group * batch < (blocks - 1) * PANEL:
                done = slice(group * batch, min((group + 1) * batch, (blocks - 1) * PANEL))
                head = a_ref[done, pl.ds(following, PANEL)]
                row = lax.broadcasted_iota(jnp.int32, head.shape, 0) + group * batch
                part = jnp.dot(
                    jnp.where(row < base, head, 0.0).T, a_ref[done, :],
                    precision=lax.Precision.HIGH, preferred_element_type=jnp.float32,
                )
                update[...] = update[...] + part if group else part
            for t in range(SUB // STRIP):
                strip = group * (SUB // STRIP) + t
                start = pl.multiple_of(base + strip * STRIP, STRIP)
                rows, sub, lanes = factor_strip(a_ref, start, panel, strip, width)
                for later in range(strip + 1, (group + 1) * (SUB // STRIP)):
                    below = pl.multiple_of(base + later * STRIP, STRIP)
                    picked = lanes == sub + later * STRIP
                    mult = [
                        jnp.sum(jnp.where(picked, rows[k][blocks], 0.0), axis=1, keepdims=True)
                        for k in range(STRIP)
                    ]
                    for b in range(blocks):
                        at = (pl.ds(below, STRIP), slice(b * PANEL, (b + 1) * PANEL))
                        terms = [mult[k] * rows[k][b] for k in range(STRIP)]
                        while len(terms) > 1:
                            terms = [x + y for x, y in zip(terms[::2], terms[1::2])]
                        a_ref[at] = a_ref[at] - terms[0]
            if group < PANEL // SUB - 1:
                done = pl.ds(pl.multiple_of(base + group * SUB, SUB), SUB)
                left = PANEL - (group + 1) * SUB
                head = a_ref[done, pl.ds(base, PANEL)].T[(group + 1) * SUB:, :]
                rest = pl.ds(pl.multiple_of(base + (group + 1) * SUB, SUB), left)
                a_ref[rest, :] = a_ref[rest, :] - jnp.dot(
                    head, a_ref[done, :], precision=lax.Precision.HIGH, preferred_element_type=jnp.float32
                )

        @pl.when(panel == last_panel)
        def _():
            send_rows()

        return carry

    lax.fori_loop(0, blocks, one_panel, 0)
    pivot_count = pivot_ref.shape[0]
    row = lax.broadcasted_iota(jnp.int32, (pivot_count, width), 0) + me * pivot_count
    pivot_ref[...] = jnp.where(
        row <= lax.broadcasted_iota(jnp.int32, (pivot_count, width), 1),
        a_ref[pl.ds(pl.multiple_of(me * pivot_count, STRIP), pivot_count), :],
        0.0,
    )
    dest_in[slots_of(front), :] = dest_ref[slots_of(front), :]
    for peer in peers:
        dest_copy(peer, peer).wait_recv()
    target = lax.broadcasted_iota(jnp.int32, (slots, PANEL), 1).astype(jnp.float32) + 1.0
    place = (dest_in[...] == target).astype(jnp.float32).T[:PR_DEV, :].astype(jnp.bfloat16)

    def arrived(j, carry):
        at = pl.ds(pl.multiple_of(j * PANEL, PANEL), PANEL)
        for peer in peers:
            row_copy(peer, peer, j).wait_recv()
        sum_ref[:, at] = one_hot_dot(place, rows_in[:, at])
        return carry

    lax.fori_loop(first_block, contrib_blocks, arrived, 0)

    for peer in peers:
        dest_copy(peer, peer).wait_send()

        def left(j, carry, peer=peer):
            row_copy(peer, peer, j).wait_send()
            return carry

        lax.fori_loop(first_block, contrib_blocks, left, 0)

    def finish(c, carry):
        @pl.when(has_right)
        def _():
            to_right(out_r, c).wait_send()

        @pl.when(has_left)
        def _():
            to_left(out_l, c).wait_send()

        return carry

    lax.fori_loop(0, chunks, finish, 0)


def front_factor(x, owners, targets, fronts, pivot_count, capacity):
    rows, width = x.shape
    packed = (width // PANEL + 1) // 2 * PANEL
    slots = fronts * capacity
    contrib_width = width - PIV
    sums = pltpu.VMEM((packed, width), jnp.float32)
    sems = pltpu.SemaphoreType.DMA((packed // CHUNK,))
    row_sems = pltpu.SemaphoreType.DMA((fronts, contrib_width // PANEL))
    dest_sems = pltpu.SemaphoreType.DMA((fronts,))
    return pl.pallas_call(
        front_kernel,
        out_shape=(
            jax.ShapeDtypeStruct((pivot_count, width), jnp.float32),
            jax.ShapeDtypeStruct((PR_DEV, contrib_width), jnp.float32),
        ),
        in_specs=[pl.BlockSpec(memory_space=pltpu.VMEM)] * 3,
        out_specs=[pl.BlockSpec(memory_space=pltpu.VMEM)] * 2,
        scratch_shapes=[pltpu.VMEM((width, width), jnp.float32), pltpu.VMEM((PANEL, width), jnp.float32)]
        + [pltpu.VMEM((slots, owners.shape[0]), jnp.bfloat16), pltpu.VMEM((slots, PANEL), jnp.float32)]
        + [pltpu.VMEM((rows, width), jnp.bfloat16)] * 2
        + [sums] * 5
        + [pltpu.VMEM((slots, contrib_width), jnp.float32)] * 2
        + [pltpu.VMEM((slots, PANEL), jnp.float32)]
        + [sems] * 4
        + [row_sems] * 2
        + [dest_sems] * 2,
        compiler_params=pltpu.CompilerParams(
            vmem_limit_bytes=48 * 1024 * 1024, collective_id=0, has_side_effects=True
        ),
        name="front_factor",
    )(x, owners, targets)


def shards(stacked, row_owner, dest_local):
    contrib_count = row_owner.shape[1]
    pivot_count = PIV // lax.axis_size("leaf")
    fronts = lax.axis_size("front")
    capacity = max(2, (2 * contrib_count + fronts - 1) // fronts)
    capacity = (capacity + STRIP - 1) // STRIP * STRIP
    pivot_part, assembled = front_factor(
        stacked[0], row_owner[0], dest_local, fronts, pivot_count, capacity
    )
    return (pivot_part[None], assembled[None])


def solution(mesh):
    return jax.shard_map(
        shards,
        mesh=mesh,
        in_specs=(P("front", "leaf", None), P("front", "leaf", None), P("front", "leaf")),
        out_specs=(P("front", "leaf", None), P("front", "leaf", None)),
        check_vma=False,
    )
```

profile of v0, /device:TPU:0, one launch (start us, length us, event | category | flops | bytes accessed | tf_op | source)
XLA Modules:
  0.0 99.4 jit_solution(13178130603997279779)
XLA Ops:
  0.6 0.8 copy.5.owner_ref
  1.4 0.0 copy-start
  1.4 2.0 %copy-done = f32[1,1024,896]{2,1,0:T(8,128)S(1)} copy-done((f32[1,1024,896]{2,1,0:T(8,128)S(1)}, f32[1,1024,896]{2,1,0:T(8,128)}, u32[]{:S(2)}) %copy-start) | copy-done | bytes 3670040
  3.5 0.0 copy-start.1
  3.5 0.7 copy-done.1
  4.1 93.9 %front_factor.1 = (f32[64,896]{1,0:T(8,128)S(1)}, f32[64,640]{1,0:T(8,128)S(1)}) custom-call(f32[1024,896]{1,0:T(8,128)S(1)} %bitcast.4, s32[160,1]{1,0:T(8,128)S(1)} %copy.5.owner_ref, s32[1,160]{1,0:T(1,128)S(1)} %copy-done.1), custom_call_target="tpu_custom_call" | custom-call | tf_op jit(solution)/shard_map/front_factor/pallas_call | solution.py:400
  98.1 0.7 copy.8
  98.8 0.7 copy.9
Async XLA Ops:
  1.4 2.0 %copy-start = (f32[1,1024,896]{2,1,0:T(8,128)S(1)}, f32[1,1024,896]{2,1,0:T(8,128)}, u32[]{:S(2)}) copy-start(f32[1,1024,896]{2,1,0:T(8,128)} %param.3) | copy-start | bytes 11010052
  3.5 0.7 copy-start.1
where the time goes:
time: 99.9 us; the launch traced here: 99.4 us
  Pallas kernels  93.9 us (94%)
  local copies, waits for them, and re-layouts  4.85 us (5%)
    pallas_call x1, Pallas kernels, front_factor(): pl.pallas_call(front_kernel, out_shape=(jax.ShapeDtypeStruct((pivot_count...  93.9 us
    unnamed x6, local copies, waits for them, and re-layouts  4.07 us

commit v1 on v0

--- a/solution.py
+++ b/solution.py
@@ -11,7 +11,7 @@
 STRIP = 8
 SUB = 32
 PANEL = 128
-CHUNK = 32
+CHUNK = 16
 MESH = pl.DeviceIdType.MESH
 
 

time: 99.9 us -> 124 us (1.24)
  Pallas kernels: 93.9 us -> 119 us
    pallas_call x1, Pallas kernels: 93.9 us -> 119 us  [front_factor(): pl.pallas_call(front_kernel, out_shape=(jax.ShapeDtypeStruct((pivot_count...]
where the time goes in v1:
time: 124 us
  Pallas kernels  119 us (96%)
  local copies, waits for them, and re-layouts  4.85 us (4%)
    pallas_call x1, Pallas kernels, front_factor(): pl.pallas_call(front_kernel, out_shape=(jax.ShapeDtypeStruct((pivot_count...  119 us
    unnamed x6, local copies, waits for them, and re-layouts  4.07 us

profile of v1, /device:TPU:0, one launch (start us, length us, event | category | flops | bytes accessed | tf_op | source)
XLA Modules:
  0.0 124.2 jit_solution(4163588809040931907)
XLA Ops:
  0.6 0.8 copy.5.owner_ref
  1.4 0.0 copy-start
  1.4 2.0 %copy-done = f32[1,1024,896]{2,1,0:T(8,128)S(1)} copy-done((f32[1,1024,896]{2,1,0:T(8,128)S(1)}, f32[1,1024,896]{2,1,0:T(8,128)}, u32[]{:S(2)}) %copy-start) | copy-done | bytes 3670040
  3.5 0.0 copy-start.1
  3.5 0.7 copy-done.1
  4.1 118.7 %front_factor.1 = (f32[64,896]{1,0:T(8,128)S(1)}, f32[64,640]{1,0:T(8,128)S(1)}) custom-call(f32[1024,896]{1,0:T(8,128)S(1)} %bitcast.4, s32[160,1]{1,0:T(8,128)S(1)} %copy.5.owner_ref, s32[1,160]{1,0:T(1,128)S(1)} %copy-done.1), custom_call_target="tpu_custom_call" | custom-call | tf_op jit(solution)/shard_map/front_factor/pallas_call | solution.py:400
  122.8 0.7 copy.8
  123.5 0.7 copy.9
Async XLA Ops:
  1.4 2.0 %copy-start = (f32[1,1024,896]{2,1,0:T(8,128)S(1)}, f32[1,1024,896]{2,1,0:T(8,128)}, u32[]{:S(2)}) copy-start(f32[1,1024,896]{2,1,0:T(8,128)} %param.3) | copy-start | bytes 11010052
  3.5 0.7 copy-start.1
